TPU v7x, 32 devices: a whole 2x2x4 slice. The times are simulated.
32 devices in a mesh: row: 8 (over z, y), col: 4 (over x, core).
Axes of the slice: x: 2, y: 2, z: 4, core: 2. Of those that a mesh axis runs over, the one named last changes fastest.
Arguments:
- epoch_a: bfloat16 [32, 512, 2048], P(None, 'row', 'col'), may hold values from -6 to 6
- epoch_b: bfloat16 [32, 512, 2048], P(None, 'row', 'col'), may hold values from -6 to 6
- sources: int32 [3, 4, 64, 1], replicated, may hold values from 0 to 7; in each aligned block of 8 rows (0 to 7, 8 to 15, ..., all dimensions but the last counted through in order) at most 2 rows name the same one
Outputs:
- volume_fine: bfloat16 [81, 512, 2048], P(None, 'row', 'col')
- volume_mid: bfloat16 [81, 256, 1024], P(None, 'row', 'col')
- volume_coarse: bfloat16 [81, 128, 512], P(None, 'row', 'col')
Inputs may be any that keep to these rules, and one draw needn't show every extreme that they name: `sources`: among the 8 row-blocks of one tile row at one level and one column tile, at most 2 name the same tile row, and 2 is reached in some of them.
All inputs are finite; a program needn't handle non-finite values.
Results may differ from a plain program's by a relative error of at most 0.0063.
Values may be sent and summed in bfloat16 or wider, within the bound.
A program may use at most 704 MiB of HBM per device.

v0:
```python
import jax
import jax.numpy as jnp
from jax import lax
from jax.sharding import PartitionSpec as P

C = 32
LEVELS = 3
CAP = 2


GAUSS_TAPS = (1.0, 4.0, 6.0, 4.0, 1.0)
TAP_ENERGY = 70.0**0.5
WINDOW_RIM = 4


def padded(x, sides, width):
    for axis, dim in sides:
        count, length = (lax.axis_size(axis), x.shape[dim])
        up = [(i, (i + 1) % count) for i in range(count - 1)]
        down = [(j, i) for i, j in up]
        last = lax.slice_in_dim(x, length - width, length, axis=dim)
        initial = lax.slice_in_dim(x, 0, width, axis=dim)
        before = lax.ppermute(last, axis, up)
        after = lax.ppermute(initial, axis, down)
        x = jnp.concatenate([before, x, after], axis=dim)
    return x


def reduce_resolution(padded_image, edge_margin, output_rows, output_columns):
    row_pass = None
    for tap_index in range(5):
        first_row = edge_margin - 2 + tap_index
        shifted = padded_image[..., first_row : first_row + 2 * output_rows : 2, :].astype(
            jnp.float32
        ) * (GAUSS_TAPS[tap_index] / TAP_ENERGY)
        row_pass = shifted if row_pass is None else row_pass + shifted
    result = None
    for tap_index in range(5):
        first_col = edge_margin - 2 + tap_index
        shifted = row_pass[..., first_col : first_col + 2 * output_columns : 2] * (
            GAUSS_TAPS[tap_index] / TAP_ENERGY
        )
        result = shifted if result is None else result + shifted
    return result.astype(jnp.bfloat16)


def correlate(features, windows):
    block_rows = features.shape[1]
    breadth = features.shape[-1]
    scaling = features.shape[0] ** (-0.5)
    planes = [None] * 81
    for col_offset in range(2 * WINDOW_RIM + 1):
        moved_cols = windows[..., col_offset : col_offset + breadth]
        for row_offset in range(2 * WINDOW_RIM + 1):
            moving = moved_cols[:, row_offset : row_offset + block_rows]
            plane = jnp.einsum(
                "crbw,crbw->rbw", features, moving, preferred_element_type=jnp.float32
            )
            planes[row_offset * 9 + col_offset] = (plane * scaling).astype(jnp.bfloat16)
    return jnp.stack(planes)


def cut_blocks(search, block_count, block_rows):
    margin = 2 * WINDOW_RIM
    pieces_needed = 1 + -(-margin // block_rows)
    columns_now = search.shape[-1]
    collected = []
    for piece_index in range(pieces_needed):
        sliced = search[
            ..., piece_index * block_rows : piece_index * block_rows + block_count * block_rows, :
        ]
        collected.append(sliced.reshape(sliced.shape[:-2] + (block_count, block_rows, columns_now)))
    joined = jnp.concatenate(collected, axis=-2)
    return jnp.swapaxes(joined, -3, -2)


def exchanged_windows(search, table, row_me, block_count, block_rows):
    row_devices = table.shape[0]
    blocks = cut_blocks(search, block_count, block_rows)
    mine = table == row_me
    ranking = jnp.cumsum(mine.astype(jnp.int32), axis=1) - 1
    slot_ids = jnp.arange(CAP, dtype=jnp.int32)
    chosen = (mine[:, None, :] & (ranking[:, None, :] == slot_ids[None, :, None])).astype(
        jnp.bfloat16
    )
    outgoing = jnp.einsum(
        "jsb,crbw->jscrw", chosen, blocks, preferred_element_type=jnp.float32
    ).astype(jnp.bfloat16)
    incoming = lax.all_to_all(outgoing, "row", split_axis=0, concat_axis=0, tiled=True)
    wanted = lax.dynamic_index_in_dim(table, row_me, 0, keepdims=False)
    same_source = wanted[:, None] == wanted[None, :]
    block_line = jnp.arange(block_count, dtype=jnp.int32)
    before = block_line[None, :] < block_line[:, None]
    order_in = jnp.sum((same_source & before).astype(jnp.int32), axis=1)
    device_line = jnp.arange(row_devices, dtype=jnp.int32)
    picker = (
        (wanted[:, None, None] == device_line[None, :, None])
        & (order_in[:, None, None] == slot_ids[None, None, :])
    ).astype(jnp.bfloat16)
    return jnp.einsum(
        "bis,iscrw->crbw", picker, incoming, preferred_element_type=jnp.float32
    ).astype(jnp.bfloat16)


def level_windows(search, table, row_me, block_count, block_rows):
    return exchanged_windows(search, table, row_me, block_count, block_rows)


def local(epoch_a, epoch_b, sources):
    row_me = lax.axis_index("row")
    col_me = lax.axis_index("col")
    row_devices = lax.axis_size("row")
    epoch_couple = jnp.stack((epoch_a, epoch_b))
    volumes = []
    for level_index in range(LEVELS):
        patch_rows = epoch_couple.shape[2]
        patch_columns = epoch_couple.shape[3]
        block_rows = patch_rows // row_devices
        last_level = level_index + 1 == LEVELS
        column_table = lax.dynamic_index_in_dim(sources[level_index], col_me, 0, keepdims=False)[
            :, 0
        ]
        table = column_table.reshape(row_devices, row_devices)
        coarser_level = epoch_couple
        search = padded(epoch_couple[1], (("row", 1), ("col", 2)), WINDOW_RIM)
        if not last_level:
            bordered_image = padded(epoch_couple, (("row", 2), ("col", 3)), 2)
            coarser_level = reduce_resolution(
                bordered_image, 2, patch_rows // 2, patch_columns // 2
            )
        windows = level_windows(search, table, row_me, row_devices, block_rows)
        features = jnp.swapaxes(
            epoch_couple[0].reshape(C, row_devices, block_rows, patch_columns), 1, 2
        )
        planes = correlate(features, windows)
        volumes.append(jnp.swapaxes(planes, 1, 2).reshape(81, patch_rows, patch_columns))
        epoch_couple = coarser_level
    return (volumes[0], volumes[1], volumes[2])


def solution(mesh):
    return jax.shard_map(
        local,
        mesh=mesh,
        in_specs=(P(None, "row", "col"), P(None, "row", "col"), P()),
        out_specs=(P(None, "row", "col"), P(None, "row", "col"), P(None, "row", "col")),
        check_vma=False,
    )
```

profile of v0, /device:TPU:0, one launch (start us, length us, event | category | flops | bytes accessed | tf_op | source)
XLA Modules:
  0.0 1443.9 jit_solution(1066357061248895202)
XLA Ops:
  6.1 4.9 collective-permute-start.4
  14.1 4.5 collective-permute-start
  42.0 7.9 pad_maximum_fusion
  49.9 4.2 multiply_add_fusion
  54.1 70.9 %slice.1267 = f32[2,32,32,256]{3,1,2,0:T(8,128)S(1)} slice(f32[2,32,32,516]{3,1,2,0:T(8,128)} %multiply_add_fusion), slice={[0:2:1], [0:32:1], [0:32:1], [0:512:2]} | slice | bytes 4194304 | tf_op jit(solution)/shard_map/slice | solution.py:40
  125.0 71.3 %slice.1268 = f32[2,32,32,256]{3,1,2,0:T(8,128)} slice(f32[2,32,32,516]{3,1,2,0:T(8,128)} %multiply_add_fusion), slice={[0:2:1], [0:32:1], [0:32:1], [1:513:2]} | slice | bytes 4194304 | tf_op jit(solution)/shard_map/slice | solution.py:40
  196.4 71.7 %slice.1269 = f32[2,32,32,256]{3,1,2,0:T(8,128)} slice(f32[2,32,32,516]{3,1,2,0:T(8,128)} %multiply_add_fusion), slice={[0:2:1], [0:32:1], [0:32:1], [2:514:2]} | slice | bytes 4194304 | tf_op jit(solution)/shard_map/slice | solution.py:40
  268.1 71.3 %slice.1270 = f32[2,32,32,256]{3,1,2,0:T(8,128)} slice(f32[2,32,32,516]{3,1,2,0:T(8,128)} %multiply_add_fusion), slice={[0:2:1], [0:32:1], [0:32:1], [3:515:2]} | slice | bytes 4194304 | tf_op jit(solution)/shard_map/slice | solution.py:40
  339.4 71.3 %slice.1271 = f32[2,32,32,256]{3,1,2,0:T(8,128)} slice(f32[2,32,32,516]{3,1,2,0:T(8,128)} %multiply_add_fusion), slice={[0:2:1], [0:32:1], [0:32:1], [4:516:2]} | slice | bytes 4194304 | tf_op jit(solution)/shard_map/slice | solution.py:40
  410.7 5.0 add_convert_fusion
  415.7 5.1 collective-permute-start.12
  422.7 5.2 collective-permute-done.13
  431.7 4.3 collective-permute-start.14
  443.1 5.4 collective-permute-start.2
  461.1 24.5 %slice.1372 = f32[2,32,16,128]{3,1,2,0:T(8,128)} slice(f32[2,32,16,260]{3,1,2,0:T(8,128)} %multiply_add_fusion.1), slice={[0:2:1], [0:32:1], [0:16:1], [0:256:2]} | slice | bytes 1048576 | tf_op jit(solution)/shard_map/slice | solution.py:40
  485.6 24.5 %slice.1373 = f32[2,32,16,128]{3,1,2,0:T(8,128)} slice(f32[2,32,16,260]{3,1,2,0:T(8,128)} %multiply_add_fusion.1), slice={[0:2:1], [0:32:1], [0:16:1], [1:257:2]} | slice | bytes 1048576 | tf_op jit(solution)/shard_map/slice | solution.py:40
  510.1 24.5 %slice.1374 = f32[2,32,16,128]{3,1,2,0:T(8,128)} slice(f32[2,32,16,260]{3,1,2,0:T(8,128)} %multiply_add_fusion.1), slice={[0:2:1], [0:32:1], [0:16:1], [2:258:2]} | slice | bytes 1048576 | tf_op jit(solution)/shard_map/slice | solution.py:40
  534.6 24.5 %slice.1375 = f32[2,32,16,128]{3,1,2,0:T(8,128)} slice(f32[2,32,16,260]{3,1,2,0:T(8,128)} %multiply_add_fusion.1), slice={[0:2:1], [0:32:1], [0:16:1], [3:259:2]} | slice | bytes 1048576 | tf_op jit(solution)/shard_map/slice | solution.py:40
  559.1 25.0 %slice.1376 = f32[2,32,16,128]{3,1,2,0:T(8,128)} slice(f32[2,32,16,260]{3,1,2,0:T(8,128)} %multiply_add_fusion.1), slice={[0:2:1], [0:32:1], [0:16:1], [4:260:2]} | slice | bytes 1048576 | tf_op jit(solution)/shard_map/slice | solution.py:40
  586.8 4.8 collective-permute-start.16
  593.2 4.2 collective-permute-done.17
  603.1 3.8 collective-permute-start.8
  615.9 4.2 copy.42
  620.1 5.5 all-to-all-start.2
  625.6 4.3 pad_maximum_fusion.1
  633.4 4.2 collective-permute-start.10
  638.9 5.5 convolution_convert_fusion
  644.5 20.3 %copy.20 = bf16[8,2,32,16,520]{4,1,3,2,0:T(2,128)(2,1)} copy(bf16[8,2,32,16,520]{4,0,3,2,1:T(8,128)(2,1)} %convolution_convert_fusion) | data formatting | bytes 17039360 | tf_op jit(solution)/shard_map/convert_element_type | solution.py:88
  671.1 9.4 copy.31
  680.5 4.5 all-to-all-done.2
  685.0 5.5 all-to-all-start.1
  690.4 3.4 fusion.182
  746.3 50.4 %all-to-all-done.1 = bf16[8,2,32,12,264]{4,1,3,2,0:T(2,128)(2,1)} async-done(((bf16[8,2,32,12,264]{4,1,3,2,0:T(2,128)(2,1)}), bf16[8,2,32,12,264]{4,1,3,2,0:T(2,128)(2,1)}, u32[]{:S(2)}, u32[]{:S(2)}) %all-to-all-start.1) | async-done | bytes 3244064 | tf_op jit(solution)/shard_map/all_to_all | solution.py:89
  796.7 5.6 all-to-all-start
  802.3 5.2 fusion.92
  820.9 3.4 multiply_reduce_fusion
  826.1 204.7 %all-to-all-done = bf16[8,2,32,16,520]{4,1,3,2,0:T(2,128)(2,1)} async-done(((bf16[8,2,32,16,520]{4,1,3,2,0:T(2,128)(2,1)}), bf16[8,2,32,16,520]{4,1,3,2,0:T(2,128)(2,1)}, u32[]{:S(2)}, u32[]{:S(2)}) %all-to-all-start) | async-done | bytes 8519712 | tf_op jit(solution)/shard_map/all_to_all | solution.py:89
  1030.8 10.1 fusion.2
  1040.9 26.6 %fusion.114 = (f32[8,8,512,32]{2,1,0,3:T(8,128)}, f32[8,8,512,32]{2,1,0,3:T(8,128)}, f32[8,8,512,32]{2,1,0,3:T(8,128)}, f32[8,8,512,32]{2,1,0,3:T(8,128)}, f32[8...) fusion(bf16[32,16,8,520]{3,2,1,0:T(8,128)(2,1)S(1)} %fusion.2), kind=kLoop, calls=%fused_computation.223 | loop fusion | flops 19922944 | bytes 119537664
  1067.6 26.6 %fusion.132 = (f32[8,8,512,32]{2,1,0,3:T(8,128)}, f32[8,8,512,32]{2,1,0,3:T(8,128)}, f32[8,8,512,32]{2,1,0,3:T(8,128)}, f32[8,8,512,32]{2,1,0,3:T(8,128)}, f32[8...) fusion(bf16[32,16,8,520]{3,2,1,0:T(8,128)(2,1)S(1)} %fusion.2), kind=kLoop, calls=%fused_computation.259 | loop fusion | flops 19922944 | bytes 119537664
  1094.2 26.7 %fusion.150 = (f32[8,8,512,32]{2,1,0,3:T(8,128)}, f32[8,8,512,32]{2,1,0,3:T(8,128)}, f32[8,8,512,32]{2,1,0,3:T(8,128)}, f32[8,8,512,32]{2,1,0,3:T(8,128)}, f32[8...) fusion(bf16[32,16,8,520]{3,2,1,0:T(8,128)(2,1)S(1)} %fusion.2), kind=kLoop, calls=%fused_computation.295 | loop fusion | flops 19922944 | bytes 119537664
  1120.9 26.9 %fusion.168 = (f32[8,8,512,32]{2,1,0,3:T(8,128)}, f32[8,8,512,32]{2,1,0,3:T(8,128)}, f32[8,8,512,32]{2,1,0,3:T(8,128)}, f32[8,8,512,32]{2,1,0,3:T(8,128)}, f32[8...) fusion(bf16[32,16,8,520]{3,2,1,0:T(8,128)(2,1)S(1)} %fusion.2), kind=kLoop, calls=%fused_computation.331 | loop fusion | flops 19922944 | bytes 119537664
  1147.8 8.5 fusion.177
  1156.3 32.5 %fusion.15 = (f32[8,8,512]{2,0,1:T(8,128)S(1)}, f32[8,8,512]{2,0,1:T(8,128)S(1)}, f32[8,8,512]{2,0,1:T(8,128)S(1)}, f32[8,8,512]{2,0,1:T(8,128)S(1)}, f32[8,8,51...) fusion(f32[8,8,512,32]{2,1,0,3:T(8,128)} %get-tuple-element.324, ...), kind=kLoop, calls=%fused_computation.102 | loop fusion | flops 19628032 | bytes 41025536 | tf_op jit(solution)/shard_map/crbw,crbw->rbw/dot_general | solution.py:56
  1194.6 53.1 %fusion.33 = (f32[8,8,512]{2,0,1:T(8,128)S(1)}, f32[8,8,512]{2,0,1:T(8,128)S(1)}, f32[8,8,512]{2,0,1:T(8,128)S(1)}, f32[8,8,512]{2,0,1:T(8,128)S(1)}, f32[8,8,51...) fusion(f32[8,8,512,32]{2,1,0,3:T(8,128)} %get-tuple-element.306, ...), kind=kLoop, calls=%fused_computation.120 | loop fusion | flops 38207488 | bytes 79953920 | tf_op jit(solution)/shard_map/crbw,crbw->rbw/dot_general | solution.py:56
  1259.2 48.6 %fusion.51 = (f32[8,8,512]{2,0,1:T(8,128)S(1)}, f32[8,8,512]{2,0,1:T(8,128)S(1)}, f32[8,8,512]{2,0,1:T(8,128)S(1)}, f32[8,8,512]{2,0,1:T(8,128)S(1)}, f32[8,8,51...) fusion(f32[8,8,512,32]{2,1,0,3:T(8,128)S(1)} %copy-done.5, ...), kind=kLoop, calls=%fused_computation.138 | loop fusion | flops 38207488 | bytes 79953920 | tf_op jit(solution)/shard_map/crbw,crbw->rbw/dot_general | solution.py:56
  1319.4 53.1 %fusion.69 = (f32[8,8,512]{2,0,1:T(8,128)S(1)}, f32[8,8,512]{2,0,1:T(8,128)S(1)}, f32[8,8,512]{2,0,1:T(8,128)S(1)}, f32[8,8,512]{2,0,1:T(8,128)S(1)}, f32[8,8,51...) fusion(f32[8,8,512,32]{2,1,0,3:T(8,128)} %get-tuple-element.270, ...), kind=kLoop, calls=%fused_computation.156 | loop fusion | flops 38207488 | bytes 79953920 | tf_op jit(solution)/shard_map/crbw,crbw->rbw/dot_general | solution.py:56
  1384.0 48.2 %fusion.87 = (f32[8,8,512]{2,0,1:T(8,128)S(1)}, f32[8,8,512]{2,0,1:T(8,128)S(1)}, f32[8,8,512]{2,0,1:T(8,128)S(1)}, f32[8,8,512]{2,0,1:T(8,128)S(1)}, f32[8,8,51...) fusion(f32[8,8,512,32]{2,1,0,3:T(8,128)} %get-tuple-element.253, ...), kind=kLoop, calls=%fused_computation.174 | loop fusion | flops 38207488 | bytes 79953920 | tf_op jit(solution)/shard_map/crbw,crbw->rbw/dot_general | solution.py:56
  (525 shorter events, 205.4 us)
Async XLA Ops:
  0.6 2.9 copy-start
  3.6 16.4 %copy-start.12 = (s32[3,4,64,1]{2,3,1,0:T(1,128)S(1)}, s32[3,4,64,1]{2,3,1,0:T(1,128)}, u32[]{:S(2)}) copy-start(s32[3,4,64,1]{2,3,1,0:T(1,128)} %param.5) | copy-start | bytes 9220
  4.7 1.3 copy-start.2
  6.1 19.2 %collective-permute-start.4 = (bf16[2,32,2,512]{3,1,2,0:T(8,128)(2,1)S(1)}, bf16[2,32,2,512]{3,1,2,0:T(8,128)(2,1)S(1)}, u32[]{:S(2)}, u32[]{:S(2)}) collective-permute-start(bf16[2,32,2,512]{3,1,2,0:T(8,128)(2,1)S(1)} %get-tuple-element.335), channel_id=1, source_target_pairs={{0,4},{4,8},{8,12},{12,16},{16,20},{20,24},{24,28},{1,5},{5,9},{9,... | collective-permute-start | bytes 393224 | tf_op jit(solution)/shard_map/ppermute | solution.py:23
  11.0 14.3 collective-permute-start.5
  14.1 425.6 %collective-permute-start = (bf16[32,4,512]{2,1,0:T(4,128)(2,1)}, bf16[32,4,512]{2,1,0:T(4,128)(2,1)S(1)}, u32[]{:S(2)}, u32[]{:S(2)}) collective-permute-start(bf16[32,4,512]{2,1,0:T(4,128)(2,1)} %get-tuple-element.341), channel_id=1, source_target_pairs={{0,4},{4,8},{8,12},{12,16},{16,20},{20,24},{24,28},{1,5},{5,9},{9,... | collective-permute-start | bytes 393224 | tf_op jit(solution)/shard_map/ppermute | solution.py:23
  18.7 421.1 %collective-permute-start.1 = (bf16[32,4,512]{2,1,0:T(4,128)(2,1)}, bf16[32,4,512]{2,1,0:T(4,128)(2,1)S(1)}, u32[]{:S(2)}, u32[]{:S(2)}) collective-permute-start(bf16[32,4,512]{2,1,0:T(4,128)(2,1)} %get-tuple-element.342), channel_id=1, source_target_pairs={{4,0},{8,4},{12,8},{16,12},{20,16},{24,20},{28,24},{5,1},{9,5},{13... | collective-permute-start | bytes 393224 | tf_op jit(solution)/shard_map/ppermute | solution.py:24
  30.8 5.8 collective-permute-start.6
  34.5 4.8 collective-permute-start.7
  410.7 11.4 copy-start.20
  415.7 24.1 %copy-start.3 = (bf16[32,64,512]{2,1,0:T(8,128)(2,1)S(1)}, bf16[32,64,512]{2,1,0:T(8,128)(2,1)}, u32[]{:S(2)}) copy-start(bf16[32,64,512]{2,1,0:T(8,128)(2,1)} %param.4) | copy-start | bytes 6291460
  415.7 7.0 collective-permute-start.12
  420.8 7.1 collective-permute-start.13
  431.7 20.1 %collective-permute-start.14 = (bf16[2,32,36,2]{2,1,3,0:T(8,128)(2,1)}, bf16[2,32,36,2]{2,1,3,0:T(8,128)(2,1)}, u32[]{:S(2)}, u32[]{:S(2)}) collective-permute-start(bf16[2,32,36,2]{2,1,3,0:T(8,128)(2,1)} %copy.33), channel_id=1, source_target_pairs={{0,1},{1,2},{2,3},{4,5},{5,6},{6,7},{8,9},{9,10},{10,11},{12,13},{... | collective-permute-start | bytes 27656 | tf_op jit(solution)/shard_map/ppermute | solution.py:23
  438.4 16.0 %collective-permute-start.15 = (bf16[2,32,36,2]{2,1,3,0:T(8,128)(2,1)}, bf16[2,32,36,2]{2,1,3,0:T(8,128)(2,1)}, u32[]{:S(2)}, u32[]{:S(2)}) collective-permute-start(bf16[2,32,36,2]{2,1,3,0:T(8,128)(2,1)} %copy.34), channel_id=1, source_target_pairs={{1,0},{2,1},{3,2},{5,4},{6,5},{7,6},{9,8},{10,9},{11,10},{13,12},{... | collective-permute-start | bytes 27656 | tf_op jit(solution)/shard_map/ppermute | solution.py:24
  443.1 163.9 %collective-permute-start.2 = (bf16[32,72,4]{1,0,2:T(8,128)(2,1)}, bf16[32,72,4]{1,0,2:T(8,128)(2,1)}, u32[]{:S(2)}, u32[]{:S(2)}) collective-permute-start(bf16[32,72,4]{1,0,2:T(8,128)(2,1)} %copy.14), channel_id=1, source_target_pairs={{0,1},{1,2},{2,3},{4,5},{5,6},{6,7},{8,9},{9,10},{10,11},{12,13},{... | collective-permute-start | bytes 55304 | tf_op jit(solution)/shard_map/ppermute | solution.py:23
  450.5 159.7 %collective-permute-start.3 = (bf16[32,72,4]{1,0,2:T(8,128)(2,1)}, bf16[32,72,4]{1,0,2:T(8,128)(2,1)}, u32[]{:S(2)}, u32[]{:S(2)}) collective-permute-start(bf16[32,72,4]{1,0,2:T(8,128)(2,1)} %copy.15), channel_id=1, source_target_pairs={{1,0},{2,1},{3,2},{5,4},{6,5},{7,6},{9,8},{10,9},{11,10},{13,12},{... | collective-permute-start | bytes 55304 | tf_op jit(solution)/shard_map/ppermute | solution.py:24
  586.8 6.4 collective-permute-start.16
  591.6 5.8 collective-permute-start.17
  593.0 14.0 copy-start.6
  593.2 13.9 copy-start.10
  597.4 9.7 copy-start.11
  598.2 13.9 collective-permute-start.18
  601.2 11.0 collective-permute-start.19
  603.1 28.3 %collective-permute-start.8 = (bf16[32,4,256]{2,0,1:T(8,128)(2,1)}, bf16[32,4,256]{2,0,1:T(8,128)(2,1)}, u32[]{:S(2)}, u32[]{:S(2)}) collective-permute-start(bf16[32,4,256]{2,0,1:T(8,128)(2,1)} %get-tuple-element.354), channel_id=1, source_target_pairs={{0,4},{4,8},{8,12},{12,16},{16,20},{20,24},{24,28},{1,5},{5,9},{9,... | collective-permute-start | bytes 196616 | tf_op jit(solution)/shard_map/ppermute | solution.py:23
  607.1 24.4 %collective-permute-start.9 = (bf16[32,4,256]{2,0,1:T(8,128)(2,1)}, bf16[32,4,256]{2,0,1:T(8,128)(2,1)}, u32[]{:S(2)}, u32[]{:S(2)}) collective-permute-start(bf16[32,4,256]{2,0,1:T(8,128)(2,1)} %get-tuple-element.355), channel_id=1, source_target_pairs={{4,0},{8,4},{12,8},{16,12},{20,16},{24,20},{28,24},{5,1},{9,5},{13... | collective-permute-start | bytes 196616 | tf_op jit(solution)/shard_map/ppermute | solution.py:24
  620.1 64.8 %all-to-all-start.2 = ((bf16[8,2,32,10,136]{4,1,3,2,0:T(2,128)(2,1)}), bf16[8,2,32,10,136]{4,1,3,2,0:T(2,128)(2,1)}, u32[]{:S(2)}, u32[]{:S(2)}) async-start(bf16[8,2,32,10,136]{4,1,3,2,0:T(2,128)(2,1)} %copy.42), calls=%async_computation.2 | async-start | bytes 5242880 | tf_op jit(solution)/shard_map/all_to_all | solution.py:89
  630.4 1.0 copy-start.7
  633.4 31.4 %collective-permute-start.10 = (bf16[32,40,4]{2,0,1:T(8,128)(2,1)}, bf16[32,40,4]{2,0,1:T(8,128)(2,1)S(1)}, u32[]{:S(2)}, u32[]{:S(2)}) collective-permute-start(bf16[32,40,4]{2,0,1:T(8,128)(2,1)} %get-tuple-element.352), channel_id=1, source_target_pairs={{0,1},{1,2},{2,3},{4,5},{5,6},{6,7},{8,9},{9,10},{10,11},{12,13},{... | collective-permute-start | bytes 30728 | tf_op jit(solution)/shard_map/ppermute | solution.py:23
  637.6 27.2 %collective-permute-start.11 = (bf16[32,40,4]{2,0,1:T(8,128)(2,1)}, bf16[32,40,4]{2,0,1:T(8,128)(2,1)}, u32[]{:S(2)}, u32[]{:S(2)}) collective-permute-start(bf16[32,40,4]{2,0,1:T(8,128)(2,1)} %get-tuple-element.353), channel_id=1, source_target_pairs={{1,0},{2,1},{3,2},{5,4},{6,5},{7,6},{9,8},{10,9},{11,10},{13,12},{... | collective-permute-start | bytes 30728 | tf_op jit(solution)/shard_map/ppermute | solution.py:24
  644.5 20.3 %copy-start.9 = (bf16[1,32,16,128]{3,1,2,0:T(8,128)(2,1)S(1)}, bf16[1,32,16,128]{3,1,2,0:T(8,128)(2,1)}, u32[]{:S(2)}) copy-start(bf16[1,32,16,128]{3,1,2,0:T(8,128)(2,1)} %get-tuple-element.361) | copy-start | bytes 393220
  644.5 20.4 %copy-start.8 = (bf16[32,32,256]{2,0,1:T(8,128)(2,1)S(1)}, bf16[32,32,256]{2,0,1:T(8,128)(2,1)}, u32[]{:S(2)}) copy-start(bf16[32,32,256]{2,0,1:T(8,128)(2,1)} %copy-done.6) | copy-start | bytes 1572868
  666.5 1.7 copy-start.13
  680.5 9.9 copy-start.15
  680.5 9.9 copy-start.19
  685.0 111.7 %all-to-all-start.1 = ((bf16[8,2,32,12,264]{4,1,3,2,0:T(2,128)(2,1)}), bf16[8,2,32,12,264]{4,1,3,2,0:T(2,128)(2,1)}, u32[]{:S(2)}, u32[]{:S(2)}) async-start(bf16[8,2,32,12,264]{4,1,3,2,0:T(2,128)(2,1)} %copy.31), calls=%async_computation.1 | async-start | bytes 9437184 | tf_op jit(solution)/shard_map/all_to_all | solution.py:89
  746.3 55.9 %copy-start.16 = (pred[8,8]{1,0:T(8,128)(4,1)S(1)}, pred[8,8]{1,0:T(8,128)(4,1)}, u32[]{:S(2)}) copy-start(pred[8,8]{1,0:T(8,128)(4,1)} %iota_compare_fusion.4) | copy-start | bytes 196
  746.3 56.0 %copy-start.18 = (pred[8,2]{0,1:T(4,128)(4,1)S(1)}, pred[8,2]{0,1:T(4,128)(4,1)}, u32[]{:S(2)}) copy-start(pred[8,2]{0,1:T(4,128)(4,1)} %iota_compare_fusion.8) | copy-start | bytes 52
  796.7 234.1 %all-to-all-start = ((bf16[8,2,32,16,520]{4,1,3,2,0:T(2,128)(2,1)}), bf16[8,2,32,16,520]{4,1,3,2,0:T(2,128)(2,1)}, u32[]{:S(2)}, u32[]{:S(2)}) async-start(bf16[8,2,32,16,520]{4,1,3,2,0:T(2,128)(2,1)} %copy.20), calls=%async_computation | async-start | bytes 20971520 | tf_op jit(solution)/shard_map/all_to_all | solution.py:89
  820.9 209.9 %copy-start.14 = (pred[8,8]{1,0:T(8,128)(4,1)S(1)}, pred[8,8]{1,0:T(8,128)(4,1)}, u32[]{:S(2)}) copy-start(pred[8,8]{1,0:T(8,128)(4,1)} %iota_compare_fusion.6) | copy-start | bytes 196
  820.9 209.9 %copy-start.17 = (pred[8,2]{0,1:T(4,128)(4,1)S(1)}, pred[8,2]{0,1:T(4,128)(4,1)}, u32[]{:S(2)}) copy-start(pred[8,2]{0,1:T(4,128)(4,1)} %iota_compare_fusion.9) | copy-start | bytes 52
  1147.7 8.5 copy-start.1
  1194.6 64.6 %copy-start.5 = (f32[8,8,512,32]{2,1,0,3:T(8,128)S(1)}, f32[8,8,512,32]{2,1,0,3:T(8,128)}, u32[]{:S(2)}) copy-start(f32[8,8,512,32]{2,1,0,3:T(8,128)} %get-tuple-element.288) | copy-start | bytes 12582916
  1319.4 64.6 %copy-start.4 = (f32[8,8,512,32]{2,1,0,3:T(8,128)S(1)}, f32[8,8,512,32]{2,1,0,3:T(8,128)}, u32[]{:S(2)}) copy-start(f32[8,8,512,32]{2,1,0,3:T(8,128)} %get-tuple-element.252) | copy-start | bytes 12582916
where the time goes:
time: 1450 us; the launch traced here: 1440 us
  local copies, waits for them, and re-layouts  608 us (42%)
  other arithmetic  464 us (32%)
  waiting for transfers between devices  269 us (19%)
  starting transfers between devices  70.7 us (5%)
  matrix products  28.7 us (2%)
    slice x10, local copies, waits for them, and re-layouts, reduce_resolution(): row_pass[..., first_col:first_col + 2 * output_columns:2]  480 us
    all_to_all x3, waiting for transfers between devices, exchanged_windows(): lax.all_to_all(outgoing, 'row', split_axis=0, concat_axis=0, tiled=True)  260 us
    dot_general x5, other arithmetic, correlate(): jnp.einsum('crbw,crbw->rbw', features, moving, preferred_element_type=jnp...  235 us
    unnamed x97, other arithmetic  185 us
    unnamed x208, local copies, waits for them, and re-layouts  54.9 us
    ppermute x10, starting transfers between devices, padded(): before = lax.ppermute(last, axis, up)  41.3 us
    convert_element_type x3, local copies, waits for them, and re-layouts, exchanged_windows(): outgoing = jnp.einsum('jsb,crbw->jscrw', chosen, blocks, preferred_elemen...  33.9 us
  transfers between devices with their start and end apart: 23, of which 7 were waited for; matrix products, arithmetic and copies ran while one was open for 47% of the time, Pallas kernels for 0%

commit v1 on v0

v1 whole, which is shorter than its diff:
```python
import jax
import jax.numpy as jnp
import numpy as np
from jax import lax
from jax.experimental import pallas as pl
from jax.experimental.pallas import tpu as pltpu
from jax.sharding import PartitionSpec as P

LEVELS = 3
GAUSS_TAPS = (1.0, 4.0, 6.0, 4.0, 1.0)
TAP_ENERGY = 70.0**0.5
WINDOW_RIM = 4
SPAN = 2 * WINDOW_RIM + 1
LANES = 128
SUBLANES = 8


def padded(x, sides, width):
    for axis, dim in sides:
        count, length = (lax.axis_size(axis), x.shape[dim])
        up = [(i, (i + 1) % count) for i in range(count - 1)]
        down = [(j, i) for i, j in up]
        last = lax.slice_in_dim(x, length - width, length, axis=dim)
        initial = lax.slice_in_dim(x, 0, width, axis=dim)
        before = lax.ppermute(last, axis, up)
        after = lax.ppermute(initial, axis, down)
        x = jnp.concatenate([before, x, after], axis=dim)
    return x


def reduce_resolution(padded_image, edge_margin, output_rows, output_columns):
    row_pass = None
    for tap_index in range(5):
        first_row = edge_margin - 2 + tap_index
        shifted = padded_image[..., first_row : first_row + 2 * output_rows : 2, :].astype(
            jnp.float32
        ) * (GAUSS_TAPS[tap_index] / TAP_ENERGY)
        row_pass = shifted if row_pass is None else row_pass + shifted
    band = np.zeros((padded_image.shape[-1], output_columns), np.float32)
    for tap_index in range(5):
        places = np.arange(output_columns)
        band[edge_margin - 2 + tap_index + 2 * places, places] = (
            GAUSS_TAPS[tap_index] / TAP_ENERGY
        )
    result = jnp.einsum(
        "ecrw,wv->ecrv",
        row_pass,
        jnp.asarray(band),
        precision=lax.Precision.HIGHEST,
        preferred_element_type=jnp.float32,
    )
    return result.astype(jnp.bfloat16)


def correlate_kernel(features_ref, windows_ref, out_ref, moved, planes):
    channels, block_rows, block_count, breadth = features_ref.shape
    extent = windows_ref.shape[-1]
    window_rows = windows_ref.shape[1]
    scaling = channels ** (-0.5)
    turn = lax.rem(extent - pl.program_id(0), extent)

    def shift(c, carry):
        flat = windows_ref[c].reshape(window_rows * block_count, extent)
        rolled = pltpu.roll(flat, turn, 1)[:, :breadth]
        moved[c] = rolled.reshape(window_rows, block_count, breadth)
        return carry

    lax.fori_loop(0, channels, shift, 0)
    group = min(block_rows, 4)
    for first in range(0, block_rows, group):
        for top in range(0, block_count, SUBLANES):
            for left in range(0, breadth, LANES):
                rows = slice(top, top + SUBLANES)
                cols = slice(left, left + LANES)

                def step(c, sums, first=first, rows=rows, cols=cols):
                    anchors = [features_ref[c, first + u, rows, cols] for u in range(group)]
                    others = [
                        moved[c, first + r, rows, cols] for r in range(group + SPAN - 1)
                    ]
                    return tuple(
                        sums[u * SPAN + dy] + anchors[u] * others[u + dy]
                        for u in range(group)
                        for dy in range(SPAN)
                    )

                zero = jnp.zeros((SUBLANES, LANES), jnp.float32)
                sums = lax.fori_loop(0, channels, step, (zero,) * (group * SPAN), unroll=8)
                for u in range(group):
                    for dy in range(SPAN):
                        start = top * block_rows + first + u
                        if block_rows == 1:
                            where = pl.ds(start, SUBLANES)
                        else:
                            where = pl.ds(start, SUBLANES, stride=block_rows)
                        planes[left // LANES, dy, where, :] = sums[u * SPAN + dy] * scaling

    for dy in range(SPAN):
        for left in range(0, breadth, LANES):
            out_ref[dy, 0, :, left : left + LANES] = planes[left // LANES, dy].astype(jnp.bfloat16)


def correlate(features, windows):
    channels, block_rows, block_count, breadth = features.shape
    rows = block_rows * block_count
    flops = 2 * SPAN * SPAN * channels * rows * breadth
    volume = pl.pallas_call(
        correlate_kernel,
        grid=(SPAN,),
        out_shape=jax.ShapeDtypeStruct((SPAN, SPAN, rows, breadth), jnp.bfloat16),
        in_specs=[
            pl.BlockSpec(features.shape, lambda i: (0, 0, 0, 0), pipeline_mode=pl.Buffered(1)),
            pl.BlockSpec(windows.shape, lambda i: (0, 0, 0, 0), pipeline_mode=pl.Buffered(1)),
        ],
        out_specs=pl.BlockSpec((SPAN, 1, rows, breadth), lambda i: (0, i, 0, 0)),
        scratch_shapes=[
            pltpu.VMEM(windows.shape[:3] + (breadth,), jnp.float32),
            pltpu.VMEM((breadth // LANES, SPAN, rows, LANES), jnp.float32),
        ],
        compiler_params=pltpu.CompilerParams(vmem_limit_bytes=50 * 1024 * 1024),
        cost_estimate=pl.CostEstimate(
            flops=flops,
            bytes_accessed=4 * (features.size + windows.size) + 2 * SPAN * SPAN * rows * breadth,
            transcendentals=0,
        ),
    )(features, windows)
    return volume.reshape(SPAN * SPAN, rows, breadth)


def level_windows(search, wanted, block_count, block_rows):
    tiles = lax.all_gather(search, "row", axis=0)
    extra = -search.shape[-1] % LANES
    pieces = []
    for k in range(block_count):
        piece = lax.dynamic_slice(
            tiles,
            (wanted[k], 0, k * block_rows, 0),
            (1, search.shape[0], block_rows + 2 * WINDOW_RIM, search.shape[-1]),
        )[0]
        pieces.append(piece.astype(jnp.float32))
    return jnp.pad(jnp.stack(pieces, axis=2), ((0, 0), (0, 0), (0, 0), (0, extra)))


def local(epoch_a, epoch_b, sources):
    row_me = lax.axis_index("row")
    col_me = lax.axis_index("col")
    row_devices = lax.axis_size("row")
    epoch_couple = jnp.stack((epoch_a, epoch_b))
    volumes = []
    for level_index in range(LEVELS):
        _, channels, patch_rows, patch_columns = epoch_couple.shape
        block_rows = patch_rows // row_devices
        column_table = lax.dynamic_index_in_dim(sources[level_index], col_me, 0, keepdims=False)[
            :, 0
        ]
        table = column_table.reshape(row_devices, row_devices)
        wanted = lax.dynamic_index_in_dim(table, row_me, 0, keepdims=False)
        features = jnp.swapaxes(
            epoch_couple[0].reshape(channels, row_devices, block_rows, patch_columns), 1, 2
        ).astype(jnp.float32)
        if level_index + 1 < LEVELS:
            bordered = padded(epoch_couple, (("row", 2), ("col", 3)), WINDOW_RIM)
            search = bordered[1]
            epoch_couple = reduce_resolution(
                bordered, WINDOW_RIM, patch_rows // 2, patch_columns // 2
            )
        else:
            search = padded(epoch_couple[1], (("row", 1), ("col", 2)), WINDOW_RIM)
        windows = level_windows(search, wanted, row_devices, block_rows)
        volumes.append(correlate(features, windows))
    return tuple(volumes)


def solution(mesh):
    return jax.shard_map(
        local,
        mesh=mesh,
        in_specs=(P(None, "row", "col"), P(None, "row", "col"), P()),
        out_specs=(P(None, "row", "col"), P(None, "row", "col"), P(None, "row", "col")),
        check_vma=False,
    )
```

time: 1450 us -> 929 us (0.64)
  local copies, waits for them, and re-layouts: 608 us -> 150 us
  other arithmetic: 464 us -> 27.1 us
  waiting for transfers between devices: 269 us -> 481 us
  Pallas kernels: 0 us -> 156 us
  between operations: 2.93 us -> 59.8 us
  starting transfers between devices: 70.7 us -> 31.4 us
  matrix products: 28.7 us -> 10.9 us
    all_gather x0 -> x3, waiting for transfers between devices: none -> 455 us  [level_windows(): tiles = lax.all_gather(search, 'row', axis=0)]
    slice x14 -> x12, local copies, waits for them, and re-layouts: 481 us -> 33.7 us  [the longest x5 26.1 us: reduce_resolution(): padded_image[..., first_row:first_row + 2 * output_rows:2, :]]
    all_to_all x3 -> x0, waiting for transfers between devices: 260 us -> none  [exchanged_windows(): lax.all_to_all(outgoing, 'row', split_axis=0, concat_axis=0, tiled=True)]
    dot_general x5 -> x0, other arithmetic: 235 us -> none  [correlate(): jnp.einsum('crbw,crbw->rbw', features, moving, preferred_element_type=jnp...]
    unnamed x97 -> x0, other arithmetic: 185 us -> none
    pallas_call x0 -> x3, Pallas kernels: none -> 156 us  [correlate(): pl.pallas_call(correlate_kernel, grid=(SPAN,), out_shape=jax.ShapeDtypeSt...]
    unnamed x208 -> x22, local copies, waits for them, and re-layouts: 54.9 us -> 1.15 us
    another operation x2 -> x4, local copies, waits for them, and re-layouts: 0.61 us -> 52.5 us  [the longest x3 47.9 us: level_windows(): jnp.stack(pieces, axis=2)]
  transfers between devices with their start and end apart: 23 -> 15, of which waited for: 7 -> 11; matrix products, arithmetic and copies ran while one was open for 47% -> 7% of each run, Pallas kernels for 0% -> 8%
where the time goes in v1:
time: 929 us; the launch traced here: 917 us
  waiting for transfers between devices  481 us (52%)
  Pallas kernels  156 us (17%)
  local copies, waits for them, and re-layouts  150 us (16%)
  between operations  59.8 us (6%)
  starting transfers between devices  31.4 us (3%)
  other arithmetic  27.1 us (3%)
  matrix products  10.9 us (1%)
    all_gather x3, waiting for transfers between devices, level_windows(): tiles = lax.all_gather(search, 'row', axis=0)  455 us
    pallas_call x3, Pallas kernels, correlate(): pl.pallas_call(correlate_kernel, grid=(SPAN,), out_shape=jax.ShapeDtypeSt...  156 us
    another operation x3, local copies, waits for them, and re-layouts, level_windows(): jnp.stack(pieces, axis=2)  47.9 us
    convert_element_type x26, local copies, waits for them, and re-layouts, level_windows(): pieces.append(piece.astype(jnp.float32))  36.6 us
    slice x5, local copies, waits for them, and re-layouts, reduce_resolution(): padded_image[..., first_row:first_row + 2 * output_rows:2, :]  26.1 us
    ppermute x6, starting transfers between devices, padded(): before = lax.ppermute(last, axis, up)  23.4 us
  transfers between devices with their start and end apart: 15, of which 11 were waited for; matrix products, arithmetic and copies ran while one was open for 7% of the time, Pallas kernels for 8%

profile of v1, /device:TPU:0, one launch (start us, length us, event | category | flops | bytes accessed | tf_op | source)
XLA Modules:
  0.0 916.6 jit_solution(5411846094355563178)
XLA Ops:
  7.2 4.6 copy_bitcast_fusion.1
  11.9 4.9 collective-permute-start
  18.0 9.8 %collective-permute-done = bf16[2,32,4,512]{3,1,2,0:T(8,128)(2,1)S(1)} collective-permute-done((bf16[2,32,4,512]{3,1,2,0:T(8,128)(2,1)S(1)}, bf16[2,32,4,512]{3,1,2,0:T(8,128)(2,1)S(1)}, u32[]{:S(2)}, u32[]{:S(2)}) %collective-permute-start) | collective-permute-done | bytes 262176 | tf_op jit(solution)/shard_map/ppermute | solution.py:25
  29.5 3.2 copy.154
  32.7 1.9 collective-permute-start.2
  34.6 2.0 copy.155
  37.9 2.7 copy.156
  41.2 3.6 copy.157
  44.8 8.5 pad_maximum_fusion
  53.4 6.8 fusion
  60.9 4.4 collective-permute-start.4
  67.8 4.9 collective-permute-done.5
  74.3 4.0 collective-permute-start.6
  81.5 1.7 collective-permute-done.7
  84.5 3.2 pad_maximum_fusion.1
  87.8 5.3 slice.220
  93.0 5.2 slice.221
  98.2 5.2 slice.222
  103.4 5.2 slice.223
  108.6 5.2 slice.224
  113.9 4.2 fusion.38
  118.1 4.8 collective-permute-start.8
  124.5 4.2 collective-permute-done.9
  129.0 3.4 collective-permute-start.10
  133.7 2.9 collective-permute-done.11
  139.2 1.8 slice-done
  141.0 2.6 copy.158
  177.4 5.8 copy.253
  199.6 2.1 all-gather.9.cloned.1.call-done
  201.7 2.5 dynamic-slice_bitcast_fusion.8
  210.6 6.9 stack.20
  217.9 28.5 %shard_map.78 = bf16[9,9,16,128]{3,2,1,0:T(8,128)(2,1)} custom-call(f32[32,2,8,128]{3,2,1,0:T(8,128)S(1)} %bitcast.115, f32[32,10,8,256]{3,2,1,0:T(8,128)S(1)} %pad_convert_fusion.2.windows_ref), custom_call_target="tpu_custom_call" | custom-call | flops 10616832 | bytes 3215360 | tf_op jit(solution)/shard_map/pallas_call | solution.py:107
  246.4 75.1 %all-gather.7.cloned.1.call-done = bf16[8,32,40,264]{3,2,1,0:T(8,128)(2,1)} async-done(((bf16[1,32,40,264]{3,2,1,0:T(8,128)(2,1)}), bf16[8,32,40,264]{3,2,1,0:T(8,128)(2,1)}) %all-gather.7.cloned.1.call-update) | async-done | bytes 5406736 | tf_op jit(solution)/shard_map/all_gather | solution.py:131
  321.5 2.8 constant_dynamic-slice_fusion.2
  335.1 14.0 %stack.19 = bf16[32,12,8,264]{3,2,1,0:T(8,128)(2,1)S(1)} concatenate(bf16[32,12,1,264]{3,2,1,0:T(2,128)(2,1)} %copy.182, bf16[32,12,1,264]{3,2,1,0:T(2,128)(2,1)} %copy.183, bf16[32,12,1,264]{3,2,1,0:T(2,128)(2,1)} %copy.184, bf16[32,12,1,264]{3,2,1,0:T(2,128)(2,1)} %copy.185, bf16[32,12,1,264]{3,2,1,0:T(2,128)(2,1)} %copy.186, bf16[32,12,1,264]{3,2,1,0:T(2,128)(2,1)} %copy.187, ...), dimensions={2} | concatenate | bytes 3244032 | tf_op jit(solution)/shard_map/stack | solution.py:141
  349.1 2.8 pad_convert_fusion.1.windows_ref
  351.9 42.5 %shard_map.77 = bf16[9,9,32,256]{3,2,1,0:T(8,128)(2,1)} custom-call(f32[32,4,8,256]{3,2,1,0:T(8,128)S(1)} %bitcast.114, f32[32,12,8,384]{3,2,1,0:T(8,128)} %pad_convert_fusion.1.windows_ref), custom_call_target="tpu_custom_call" | custom-call | flops 42467328 | bytes 7094272 | tf_op jit(solution)/shard_map/pallas_call | solution.py:107
  394.4 377.8 %all-gather.5.cloned.1.call-done = bf16[8,32,72,520]{3,2,1,0:T(8,128)(2,1)} async-done(((bf16[1,32,72,520]{3,2,1,0:T(8,128)(2,1)}), bf16[8,32,72,520]{3,2,1,0:T(8,128)(2,1)}) %all-gather.5.cloned.1.call-update) | async-done | bytes 19169296 | tf_op jit(solution)/shard_map/all_gather | solution.py:131
  772.2 3.0 dynamic-slice_bitcast_fusion
  777.2 2.1 copy.161
  779.3 2.1 copy.162
  781.4 2.1 copy.163
  783.5 2.1 copy.164
  785.6 2.1 copy.165
  787.7 2.1 copy.166
  789.8 26.9 %stack.18 = bf16[32,16,8,520]{3,2,1,0:T(8,128)(2,1)} concatenate(bf16[32,16,1,520]{3,2,1,0:T(2,128)(2,1)S(1)} %copy.159, bf16[32,16,1,520]{3,2,1,0:T(2,128)(2,1)S(1)} %copy.160, bf16[32,16,1,520]{3,2,1,0:T(2,128)(2,1)} %copy.161, bf16[32,16,1,520]{3,2,1,0:T(2,128)(2,1)} %copy.162, bf16[32,16,1,520]{3,2,1,0:T(2,128)(2,1)} %copy.163, bf16[32,16,1,520]{3,2,1,0:T(2,128)(2,1)} %copy.164, ...), dimensions={2} | concatenate | bytes 8519680 | tf_op jit(solution)/shard_map/stack | solution.py:141
  816.7 7.8 pad_convert_fusion.windows_ref
  824.5 85.1 %shard_map.76 = bf16[9,9,64,512]{3,2,1,0:T(8,128)(2,1)} custom-call(f32[32,8,8,512]{3,2,1,0:T(8,128)} %bitcast.116, f32[32,16,8,640]{3,2,1,0:T(8,128)} %pad_convert_fusion.windows_ref), custom_call_target="tpu_custom_call" | custom-call | flops 169869312 | bytes 19988480 | tf_op jit(solution)/shard_map/pallas_call | solution.py:107
  (94 shorter events, 44.1 us)
Async XLA Ops:
  7.2 194.6 %all-gather.9.cloned.1.call-start = ((), (), s32[]{:S(2)}) async-start(), calls=%async_computation.2 | async-start | bytes 3538944 | tf_op jit(solution)/shard_map/all_gather | solution.py:131
  11.8 16.1 %copy-start = (bf16[1,32,64,512]{3,1,2,0:T(8,128)(2,1)}, bf16[1,32,64,512]{3,1,2,0:T(8,128)(2,1)S(1)}, u32[]{:S(2)}) copy-start(bf16[1,32,64,512]{3,1,2,0:T(8,128)(2,1)S(1)} %get-tuple-element.69) | copy-start | bytes 6291460
  11.9 16.0 %collective-permute-start = (bf16[2,32,4,512]{3,1,2,0:T(8,128)(2,1)S(1)}, bf16[2,32,4,512]{3,1,2,0:T(8,128)(2,1)S(1)}, u32[]{:S(2)}, u32[]{:S(2)}) collective-permute-start(bf16[2,32,4,512]{3,1,2,0:T(8,128)(2,1)S(1)} %get-tuple-element.21), channel_id=1, source_target_pairs={{0,4},{4,8},{8,12},{12,16},{16,20},{20,24},{24,28},{1,5},{5,9},{9,... | collective-permute-start | bytes 786440 | tf_op jit(solution)/shard_map/ppermute | solution.py:25
  16.7 11.2 %collective-permute-start.1 = (bf16[2,32,4,512]{3,1,2,0:T(8,128)(2,1)S(1)}, bf16[2,32,4,512]{3,1,2,0:T(8,128)(2,1)S(1)}, u32[]{:S(2)}, u32[]{:S(2)}) collective-permute-start(bf16[2,32,4,512]{3,1,2,0:T(8,128)(2,1)S(1)} %get-tuple-element.22), channel_id=1, source_target_pairs={{4,0},{8,4},{12,8},{16,12},{20,16},{24,20},{28,24},{5,1},{9,5},{13... | collective-permute-start | bytes 786440 | tf_op jit(solution)/shard_map/ppermute | solution.py:26
  27.9 1.6 copy-start.3
  32.7 5.1 collective-permute-start.2
  36.6 4.6 collective-permute-start.3
  44.8 8.6 copy-start.5
  53.4 6.8 copy-start.1
  60.9 6.9 collective-permute-start.4
  65.3 7.4 collective-permute-start.5
  74.3 5.8 collective-permute-start.6
  78.9 4.3 collective-permute-start.7
  98.2 15.7 %copy-start.6 = (f32[264,128,1,1]{1,0,3,2:T(8,128)S(1)}, f32[264,128,1,1]{1,0,3,2:T(8,128)}, u32[]{:S(2)}) copy-start(f32[264,128,1,1]{1,0,3,2:T(8,128)} %constant.85) | copy-start | bytes 405508
  118.1 6.4 collective-permute-start.8
  122.9 5.8 collective-permute-start.9
  129.0 4.7 collective-permute-start.10
  132.4 4.2 collective-permute-start.11
  137.8 183.7 %all-gather.7.cloned.1.call-start = ((), (), s32[]{:S(2)}) async-start(), calls=%async_computation.1 | async-start | bytes 8847360 | tf_op jit(solution)/shard_map/all_gather | solution.py:131
  138.9 633.3 %all-gather.5.cloned.1.call-start = ((), (), s32[]{:S(2)}) async-start(), calls=%async_computation | async-start | bytes 26542080 | tf_op jit(solution)/shard_map/all_gather | solution.py:131
  139.2 1.8 slice-start
  143.6 0.7 copy-start.4
  143.6 33.2 %copy-start.2 = (bf16[32,64,512]{2,1,0:T(8,128)(2,1)S(1)}, bf16[32,64,512]{2,1,0:T(8,128)(2,1)}, u32[]{:S(2)}) copy-start(bf16[32,64,512]{2,1,0:T(8,128)(2,1)} %param.5) | copy-start | bytes 6291460
Sparse Core Ops, SparseCore 0:
  137.9 63.7 all-gather.8
  204.5 116.9 all-gather.6
  323.1 449.1 all-gather.4
